TPU v7x, 32 devices: a whole 2x2x4 slice. The times are simulated.
32 devices in a mesh: case: 2 (over y), panel: 4 (over z), slab: 2 (over x), obs: 2 (over core).
Axes of the slice: x: 2, y: 2, z: 4, core: 2. Of those that a mesh axis runs over, the one named last changes fastest.
Arguments:
- loading: bfloat16 [65536, 512], P(('case', 'panel'), 'slab'), parts along dimension 0, may hold values from -6 to 6
- green: bfloat16 [128, 32768], P(('case', 'obs'), 'panel'), parts along dimension 0, may hold values from -0.03125 to 0.03125
- delays: int32 [128, 2048], P(('case', 'obs'), 'panel'), parts along dimension 0, may hold values from 0 to 120
- offsets: int32 [128, 2048], P(('case', 'obs'), 'panel'), parts along dimension 0, may hold values from 0 to 7
- live_groups: int32 [8], P('case'), parts along dimension 0, may hold values from 1 to 4, as said below
Outputs:
- signal: float32 [128, 512], P(('case', 'obs'), 'slab'), parts along dimension 0
There are 2 independent parts, one for each index of `case`. A program takes and returns all parts, laid end to end along the dimension named above; each array names one. Nothing has to cross between parts.
Inputs may be any that keep to these rules, and one draw needn't show every extreme that they name: `live_groups`: in every draw some sector has all 4 groups live while the sector 4/2 positions away has one.
All inputs are finite; a program needn't handle non-finite values.
Results may differ from a plain program's by a relative error of at most 0.0034.
Values may be sent and summed in bfloat16 or wider, within the bound.
No kernel may reach another device: no remote copies, remote signals or barrier semaphores. Data moves between devices by JAX's collectives and lax.ppermute only.
A program may use at most 64 MiB of HBM per device.

v0:
```python
import jax
import jax.numpy as jnp
from jax import lax
from jax.sharding import PartitionSpec as P

BP = 16
GB = 128
LAGS = 128


def passed_along(block, axis, distance):
    devices = range(lax.axis_size(axis))
    route = [(i - distance, i) for i in devices if i - distance in devices]
    return lax.ppermute(block, axis, route)


def lagrange_weights(offset_part):
    position = 3.0 + offset_part.astype(jnp.float32) / 8.0
    weights = []
    for tap in range(8):
        factor = jnp.ones_like(position)
        for other in range(8):
            if other != tap:
                factor = factor * (position - other) / (tap - other)
        weights.append(factor)
    return weights


def build_table(delay_part, offset_part, lag_count):
    lag_index = jnp.arange(lag_count, dtype=jnp.int32)[None, :, None]
    relative = lag_index - delay_part[:, None, :]
    weights = lagrange_weights(offset_part)
    table_sum = jnp.zeros(relative.shape, jnp.float32)
    for tap in range(8):
        table_sum = table_sum + jnp.where(relative == tap, weights[tap][:, None, :], 0.0)
    return table_sum.astype(jnp.bfloat16)


def skew_sum(lagged):
    observers, lag_count, samples = lagged.shape
    row_width = samples + lag_count + 1
    padded = jnp.pad(lagged, ((0, 0), (0, 0), (0, lag_count + 1)))
    flattened = padded.reshape(observers, lag_count * row_width)[:, : lag_count * (row_width - 1)]
    return flattened.reshape(observers, lag_count, row_width - 1).sum(axis=1)


def group_signal(load_part, green_part, delay_part, offset_part):
    samples = load_part.shape[1]
    observers = green_part.shape[0]
    blocked_load = load_part.reshape(GB, BP, samples)
    blocked_green = green_part.reshape(observers, GB, BP)
    block_signal = jnp.einsum(
        "obp,bpt->bot", blocked_green, blocked_load, preferred_element_type=jnp.float32
    ).astype(jnp.bfloat16)
    lag_table = build_table(delay_part, offset_part, LAGS)
    lagged = jnp.einsum("olb,bot->olt", lag_table, block_signal, preferred_element_type=jnp.float32)
    return skew_sum(lagged)


def shards(loading, green, delays, offsets, live_groups):
    samples = loading.shape[1]
    observers = green.shape[0]
    group_panels = GB * BP
    own_index = lax.axis_index("panel")
    own_count = live_groups[own_index]

    def slice_group(group):
        start = group * group_panels
        return (
            lax.dynamic_slice_in_dim(loading, start, group_panels, 0),
            lax.dynamic_slice_in_dim(green, start, group_panels, 1),
            lax.dynamic_slice_in_dim(delays, group * GB, GB, 1),
            lax.dynamic_slice_in_dim(offsets, group * GB, GB, 1),
        )

    def add_group(group, summed):
        pieces = slice_group(group)
        return summed + group_signal(pieces[0], pieces[1], pieces[2], pieces[3])

    start_sum = jnp.zeros((observers, samples + LAGS), jnp.float32)
    summed = lax.fori_loop(0, own_count, add_group, start_sum)
    carried = passed_along(summed[:, samples:], "slab", 1)
    local_part = summed[:, :samples] + jnp.pad(carried, ((0, 0), (0, samples - LAGS)))
    signal = lax.psum(local_part, "panel")
    return signal


def solution(mesh):
    placed = (
        P(("case", "panel"), "slab"),
        P(("case", "obs"), "panel"),
        P(("case", "obs"), "panel"),
        P(("case", "obs"), "panel"),
        P("case"),
    )
    return jax.shard_map(
        shards, mesh=mesh, in_specs=placed, out_specs=P(("case", "obs"), "slab"), check_vma=False
    )
```

profile of v0, /device:TPU:0, one launch (start us, length us, event | category | flops | bytes accessed | tf_op | source)
XLA Modules:
  0.0 134.4 jit_solution(11575538647123839793)
XLA Ops:
  0.0 1.3 dynamic_slice.39
  1.3 80.3 %while.14 = (s32[]{:T(128)}, f32[32,384]{1,0:T(8,128)S(1)}, s32[]{:T(128)}, s32[32,512]{1,0:T(8,128)}, s32[32,512]{1,0:T(8,128)}, /*index=5*/bf16[32,8192]{1,0:T...) while((s32[]{:T(128)}, f32[32,384]{1,0:T(8,128)S(1)}, ...), condition=%wide.region_2.3_spmd, body=%wide.region_0.2_spmd.sunk | while | flops 317104128 | bytes 73580824 | solution.py:81
  2.0 0.7 constant_dynamic-slice_fusion.8
  2.8 0.8 multiply_multiply_fusion.9
  3.5 0.9 constant_dynamic-slice_fusion.6
  4.5 0.3 copy.16
  4.8 1.3 constant_dynamic-slice_fusion.7
  6.1 0.8 fusion.45
  6.8 3.5 %fusion.46 = f32[32,128,256]{2,1,0:T(8,128)S(1)} fusion(bf16[128,32,256]{2,1,0:T(8,128)(2,1)S(1)} %fusion.45, f32[32,128]{1,0:T(8,128)S(1)} %get-tuple-element.246, f32[32,128]{1,0:T(8,128)S(1)} %get-tuple-element.247, f32[32,128]{1,0:T(8,128)S(1)} %get-tuple-element.248, f32[32,128]{1,0:T(8,128)S(1)} %get-tuple-element.249, ...), kind=kOutput, calls=%fused_computation.2.clone.1 | convolution fusion | flops 281542656 | bytes 6438912 | tf_op jit(solution)/shard_map/while/body/olb,bot->olt/dot_general | solution.py:56
  10.3 4.4 %pad.17 = f32[32,128,385]{2,1,0:T(8,128)} pad(f32[32,128,256]{2,1,0:T(8,128)S(1)} %fusion.46, f32[]{:T(128)} %constant.358.clone.1..sunk), padding=0_0x0_0x0_129 | pad | bytes 10502148 | tf_op jit(solution)/shard_map/while/body/jit(_pad)/pad | solution.py:42
  14.8 8.4 %reshape.46 = f32[32,49280]{1,0:T(8,128)} reshape(f32[32,128,385]{2,1,0:T(8,128)} %pad.17) | data formatting | bytes 12615680 | tf_op jit(solution)/shard_map/while/body/reshape | solution.py:43
  23.1 0.0 slice-start
  23.1 2.8 %slice-done = f32[32,49152]{1,0:T(8,128)S(1)} async-done(((f32[32,49280]{1,0:T(8,128)}), f32[32,49152]{1,0:T(8,128)S(1)}, s32[]{:S(2)}) %slice-start) | async-done | bytes 6291480 | tf_op jit(solution)/shard_map/while/body/slice | solution.py:43
  25.9 1.1 copy.17
  27.0 0.8 bitcast_reduce_fusion.2
  28.6 0.7 constant_dynamic-slice_fusion.8
  29.3 0.8 multiply_multiply_fusion.9
  30.1 0.9 constant_dynamic-slice_fusion.6
  31.0 0.3 copy.16
  31.3 1.3 constant_dynamic-slice_fusion.7
  32.6 0.8 fusion.45
  33.4 3.5 %fusion.46 = f32[32,128,256]{2,1,0:T(8,128)S(1)} fusion(bf16[128,32,256]{2,1,0:T(8,128)(2,1)S(1)} %fusion.45, f32[32,128]{1,0:T(8,128)S(1)} %get-tuple-element.246, f32[32,128]{1,0:T(8,128)S(1)} %get-tuple-element.247, f32[32,128]{1,0:T(8,128)S(1)} %get-tuple-element.248, f32[32,128]{1,0:T(8,128)S(1)} %get-tuple-element.249, ...), kind=kOutput, calls=%fused_computation.2.clone.1 | convolution fusion | flops 281542656 | bytes 6438912 | tf_op jit(solution)/shard_map/while/body/olb,bot->olt/dot_general | solution.py:56
  36.9 4.4 %pad.17 = f32[32,128,385]{2,1,0:T(8,128)} pad(f32[32,128,256]{2,1,0:T(8,128)S(1)} %fusion.46, f32[]{:T(128)} %constant.358.clone.1..sunk), padding=0_0x0_0x0_129 | pad | bytes 10502148 | tf_op jit(solution)/shard_map/while/body/jit(_pad)/pad | solution.py:42
  41.3 8.4 %reshape.46 = f32[32,49280]{1,0:T(8,128)} reshape(f32[32,128,385]{2,1,0:T(8,128)} %pad.17) | data formatting | bytes 12615680 | tf_op jit(solution)/shard_map/while/body/reshape | solution.py:43
  49.7 0.0 slice-start
  49.7 2.8 %slice-done = f32[32,49152]{1,0:T(8,128)S(1)} async-done(((f32[32,49280]{1,0:T(8,128)}), f32[32,49152]{1,0:T(8,128)S(1)}, s32[]{:S(2)}) %slice-start) | async-done | bytes 6291480 | tf_op jit(solution)/shard_map/while/body/slice | solution.py:43
  52.4 1.1 copy.17
  53.6 0.8 bitcast_reduce_fusion.2
  55.1 0.7 constant_dynamic-slice_fusion.8
  55.9 0.8 multiply_multiply_fusion.9
  56.6 0.9 constant_dynamic-slice_fusion.6
  57.6 0.3 copy.16
  57.8 1.3 constant_dynamic-slice_fusion.7
  59.1 0.8 fusion.45
  59.9 3.5 %fusion.46 = f32[32,128,256]{2,1,0:T(8,128)S(1)} fusion(bf16[128,32,256]{2,1,0:T(8,128)(2,1)S(1)} %fusion.45, f32[32,128]{1,0:T(8,128)S(1)} %get-tuple-element.246, f32[32,128]{1,0:T(8,128)S(1)} %get-tuple-element.247, f32[32,128]{1,0:T(8,128)S(1)} %get-tuple-element.248, f32[32,128]{1,0:T(8,128)S(1)} %get-tuple-element.249, ...), kind=kOutput, calls=%fused_computation.2.clone.1 | convolution fusion | flops 281542656 | bytes 6438912 | tf_op jit(solution)/shard_map/while/body/olb,bot->olt/dot_general | solution.py:56
  63.4 4.4 %pad.17 = f32[32,128,385]{2,1,0:T(8,128)} pad(f32[32,128,256]{2,1,0:T(8,128)S(1)} %fusion.46, f32[]{:T(128)} %constant.358.clone.1..sunk), padding=0_0x0_0x0_129 | pad | bytes 10502148 | tf_op jit(solution)/shard_map/while/body/jit(_pad)/pad | solution.py:42
  67.8 8.4 %reshape.46 = f32[32,49280]{1,0:T(8,128)} reshape(f32[32,128,385]{2,1,0:T(8,128)} %pad.17) | data formatting | bytes 12615680 | tf_op jit(solution)/shard_map/while/body/reshape | solution.py:43
  76.2 0.0 slice-start
  76.2 2.8 %slice-done = f32[32,49152]{1,0:T(8,128)S(1)} async-done(((f32[32,49280]{1,0:T(8,128)}), f32[32,49152]{1,0:T(8,128)S(1)}, s32[]{:S(2)}) %slice-start) | async-done | bytes 6291480 | tf_op jit(solution)/shard_map/while/body/slice | solution.py:43
  79.0 1.1 copy.17
  80.1 0.8 bitcast_reduce_fusion.2
  81.7 4.8 %collective-permute-start = (f32[32,128]{1,0:T(8,128)S(1)}, f32[32,128]{1,0:T(8,128)S(1)}, u32[]{:S(2)}, u32[]{:S(2)}) collective-permute-start(f32[32,128]{1,0:T(8,128)S(1)} %slice.16), channel_id=1, source_target_pairs={{0,2},{1,3},{4,6},{5,7},{8,10},{9,11},{12,14},{13,15},{16,18},{17,... | collective-permute-start | bytes 49160 | tf_op jit(solution)/shard_map/ppermute | solution.py:14
  86.5 1.4 %collective-permute-done = f32[32,128]{1,0:T(8,128)S(1)} collective-permute-done((f32[32,128]{1,0:T(8,128)S(1)}, f32[32,128]{1,0:T(8,128)S(1)}, u32[]{:S(2)}, u32[]{:S(2)}) %collective-permute-start) | collective-permute-done | bytes 16416 | tf_op jit(solution)/shard_map/ppermute | solution.py:14
  87.9 46.4 %psum.7 = f32[32,256]{1,0:T(8,128)} all-reduce(f32[32,256]{1,0:T(8,128)S(1)} %pad_add_fusion), channel_id=1, replica_groups=mesh['case'=2,'panel'=4,'slab'=2,'obs'=2] {'panel'}, use_global_device_ids=true, to_apply=%region_3.4 | all-reduce | flops 8192 | bytes 65536 | tf_op jit(solution)/shard_map/psum | solution.py:84
  (6 shorter events, 0.0 us)
Async XLA Ops:
  23.1 2.8 %slice-start = ((f32[32,49280]{1,0:T(8,128)}), f32[32,49152]{1,0:T(8,128)S(1)}, s32[]{:S(2)}) async-start(f32[32,49280]{1,0:T(8,128)} %reshape.46), calls=%async_computation | async-start | bytes 12582912 | tf_op jit(solution)/shard_map/while/body/slice | solution.py:43
  49.7 2.8 %slice-start = ((f32[32,49280]{1,0:T(8,128)}), f32[32,49152]{1,0:T(8,128)S(1)}, s32[]{:S(2)}) async-start(f32[32,49280]{1,0:T(8,128)} %reshape.46), calls=%async_computation | async-start | bytes 12582912 | tf_op jit(solution)/shard_map/while/body/slice | solution.py:43
  76.2 2.8 %slice-start = ((f32[32,49280]{1,0:T(8,128)}), f32[32,49152]{1,0:T(8,128)S(1)}, s32[]{:S(2)}) async-start(f32[32,49280]{1,0:T(8,128)} %reshape.46), calls=%async_computation | async-start | bytes 12582912 | tf_op jit(solution)/shard_map/while/body/slice | solution.py:43
  81.7 6.3 %collective-permute-start = (f32[32,128]{1,0:T(8,128)S(1)}, f32[32,128]{1,0:T(8,128)S(1)}, u32[]{:S(2)}, u32[]{:S(2)}) collective-permute-start(f32[32,128]{1,0:T(8,128)S(1)} %slice.16), channel_id=1, source_target_pairs={{0,2},{1,3},{4,6},{5,7},{8,10},{9,11},{12,14},{13,15},{16,18},{17,... | collective-permute-start | bytes 49160 | tf_op jit(solution)/shard_map/ppermute | solution.py:14
where the time goes:
time: 135 us; the launch traced here: 134 us
  local copies, waits for them, and re-layouts  61 us (45%)
  blocking collectives  46.4 us (34%)
  matrix products  12.8 us (9%)
  other arithmetic  4.86 us (4%)
  starting transfers between devices  4.84 us (4%)
  loops' own time  2.97 us (2%)
  waiting for transfers between devices  1.43 us (1%)
    psum x1, blocking collectives, shards(): signal = lax.psum(local_part, 'panel')  46.4 us
    reshape x3, local copies, waits for them, and re-layouts, skew_sum(): padded.reshape(observers, lag_count * row_width)  25.1 us
    pad x3, local copies, waits for them, and re-layouts, skew_sum(): padded = jnp.pad(lagged, ((0, 0), (0, 0), (0, lag_count + 1)))  13.3 us
    dot_general x3, matrix products, group_signal(): jnp.einsum('olb,bot->olt', lag_table, block_signal, preferred_element_typ...  10.5 us
    slice x6, local copies, waits for them, and re-layouts, skew_sum(): padded.reshape(observers, lag_count * row_width)  8.35 us
    ppermute x1, starting transfers between devices, passed_along(): return lax.ppermute(block, axis, route)  4.84 us
    dynamic_slice x3, local copies, waits for them, and re-layouts, slice_group(): lax.dynamic_slice_in_dim(loading, start, group_panels, 0)  3.9 us
    dynamic_slice x6, local copies, waits for them, and re-layouts, slice_group(): lax.dynamic_slice_in_dim(green, start, group_panels, 1)  3.58 us
  transfers between devices with their start and end apart: 1, of which 1 were waited for; matrix products, arithmetic and copies ran while one was open for 0% of the time, Pallas kernels for 0%

commit v1 on v0

v1 whole, which is shorter than its diff:
```python
import functools

import jax
import jax.numpy as jnp
from jax import lax
from jax.experimental import pallas as pl
from jax.experimental.pallas import tpu as pltpu
from jax.sharding import PartitionSpec as P

BP = 16
GB = 128
LAGS = 128
TAPS = 8
ROWS = 16
LANES = 128
CHUNK = 256


def passed_along(block, axis, distance):
    devices = range(lax.axis_size(axis))
    route = [(i - distance, i) for i in devices if i - distance in devices]
    return lax.ppermute(block, axis, route)


def weight_lanes():
    lane = lax.broadcasted_iota(jnp.int32, (8, LANES), 1)
    tap = (lane % ROWS).astype(jnp.float32)
    position = 3.0 + (lane // ROWS).astype(jnp.float32) / 8.0
    top = jnp.ones_like(position)
    bottom = jnp.ones_like(position)
    for other in range(TAPS):
        here = tap == other
        top = top * jnp.where(here, 1.0, position - other)
        bottom = bottom * jnp.where(here, 1.0, tap - other)
    return jnp.where(tap < TAPS, top / bottom, 0.0)


def shifted_add(upper, lower, distance):
    lane = lax.broadcasted_iota(jnp.int32, (8, LANES), 1)
    rows = lower[0].shape[0]
    wraps = (lane < distance)[None]
    turned = [pltpu.roll(tile, distance, 1).reshape(rows // 8, 8, LANES) for tile in lower]
    zero = jnp.zeros((rows // 8, 8, LANES), jnp.float32)
    out = []
    for at in range(max(len(upper), len(lower) + 1)):
        before = turned[at - 1] if 0 < at <= len(turned) else zero
        here = turned[at] if at < len(turned) else zero
        moved = jnp.where(wraps, before, here).reshape(rows, LANES)
        out.append(moved + upper[at] if at < len(upper) else moved)
    return out


def far_kernel(groups, live_hbm, load_hbm, green_hbm, delay_hbm, offset_hbm, main_ref, tail_ref,
               live_s, load_v, green_v, green_f, delay_v, offset_v, taps_v, place_v, sig_v, part_v,
               small_sem, load_sem):
    observers = green_v.shape[0]
    samples = load_v.shape[1]
    panels = load_v.shape[0]
    blocks = panels // BP
    pieces = load_sem.shape[0]
    piece = panels // pieces
    pairs = groups // 2
    chunk_blocks = CHUNK // BP

    small = [
        pltpu.make_async_copy(src, dst, small_sem.at[i])
        for i, (src, dst) in enumerate(
            [(live_hbm, live_s), (delay_hbm, delay_v), (offset_hbm, offset_v), (green_hbm, green_v)]
        )
    ]
    for copy in small:
        copy.start()
    loads = [
        pltpu.make_async_copy(load_hbm.at[pl.ds(i * piece, piece)], load_v.at[pl.ds(i * piece, piece)], load_sem.at[i])
        for i in range(pieces)
    ]
    for copy in loads:
        copy.start()

    weights = weight_lanes()
    for copy in small[:3]:
        copy.wait()
    count = live_s[lax.axis_index("panel")]
    live_pairs = (count + 1) // 2

    row = lax.broadcasted_iota(jnp.int32, (ROWS, LANES), 0)

    def prepare(band, carry):
        rows = pl.ds(pl.multiple_of(band * 8, 8), 8)
        for g in range(groups):
            cols = pl.ds(g * LANES, LANES)
            dead = jnp.where(g < count, 0, -1024)
            delays = delay_v[rows, cols]
            offsets = offset_v[rows, cols]
            for r in range(8):
                o = band * 8 + r
                delay = jnp.broadcast_to(delays[r:r + 1], (ROWS, LANES))
                offset = jnp.broadcast_to(offsets[r:r + 1], (ROWS, LANES))
                entry = ((row - delay) & (ROWS - 1)) + offset * ROWS
                values = [jnp.take_along_axis(weights, entry[h:h + 8], axis=1) for h in (0, 8)]
                taps_v[o, :, cols] = jnp.concatenate(values, 0).astype(jnp.bfloat16)
                place = ((delay - row + (ROWS - 1)) >> 4) + dead
                place_v[o, :, cols] = place.astype(jnp.float32).astype(jnp.bfloat16)
        return carry

    lax.fori_loop(0, observers // 8, prepare, 0)

    small[3].wait()
    for c in range(panels // CHUNK):
        green_f[c] = green_v[:, c * CHUNK:(c + 1) * CHUNK].astype(jnp.float32)
    for copy in loads:
        copy.wait()

    own = lax.broadcasted_iota(jnp.int32, (ROWS, CHUNK), 1) // BP == lax.broadcasted_iota(jnp.int32, (ROWS, CHUNK), 0)
    own = own.astype(jnp.float32).astype(jnp.bfloat16)

    def first(c, carry):
        spread = []
        for o in range(observers):
            line = jnp.broadcast_to(green_f[c, o:o + 1, :], (ROWS, CHUNK)).astype(jnp.bfloat16)
            spread.append(line * own)
        block = jnp.dot(
            jnp.concatenate(spread, 0),
            load_v[pl.ds(pl.multiple_of(c * CHUNK, CHUNK), CHUNK), :],
            preferred_element_type=jnp.float32,
        ).astype(jnp.bfloat16)
        at = pl.ds(pl.multiple_of(c * chunk_blocks, chunk_blocks), chunk_blocks)
        for o in range(observers):
            sig_v[o, at, :] = block[o * ROWS:(o + 1) * ROWS]
        return carry

    lax.fori_loop(0, live_pairs * (2 * GB // chunk_blocks), first, 0)

    def second(depth, o, carry):
        taps = taps_v[o, :, :depth]
        place = place_v[o, :, :depth]
        table = jnp.concatenate(
            [jnp.where(place == jnp.bfloat16(j), taps, jnp.bfloat16(0)) for j in range(LAGS // ROWS)], 0
        )
        lagged = jnp.dot(table, sig_v[o, :depth, :], preferred_element_type=jnp.float32)
        tiles = [lagged[:, t * LANES:(t + 1) * LANES] for t in range(samples // LANES)]
        half = LAGS // 2
        while half >= 8:
            tiles = shifted_add([t[:half] for t in tiles], [t[half:] for t in tiles], half)[: samples // LANES + 1]
            half //= 2
        for t, tile in enumerate(tiles):
            part_v[t, pl.ds(pl.multiple_of(o * 8, 8), 8), :] = tile
        return carry

    for pair in range(1, pairs + 1):
        @pl.when(live_pairs == pair)
        def _():
            lax.fori_loop(0, observers, functools.partial(second, pair * 2 * GB), 0, unroll=2)

    tiles_out = samples // LANES + 1
    total = [part_v[t, pl.ds(0, observers, stride=8), :] for t in range(tiles_out)]
    for s in range(1, 8):
        line = [part_v[t, pl.ds(s, observers, stride=8), :] for t in range(tiles_out)]
        total = shifted_add(total, line, s)[:tiles_out]
    for t in range(samples // LANES):
        main_ref[:, t * LANES:(t + 1) * LANES] = total[t]
    tail_ref[...] = total[-1]


def far_partial(loading, green, delays, offsets, live_groups):
    panels, samples = loading.shape
    observers = green.shape[0]
    blocks = panels // BP
    groups = blocks // GB
    pieces = panels // CHUNK // 2
    far = pl.BlockSpec(memory_space=pltpu.HBM)
    vmem = pl.BlockSpec(memory_space=pltpu.VMEM)
    return pl.pallas_call(
        functools.partial(far_kernel, groups),
        out_shape=(
            jax.ShapeDtypeStruct((observers, samples), jnp.float32),
            jax.ShapeDtypeStruct((observers, LAGS), jnp.float32),
        ),
        in_specs=[far] * 5,
        out_specs=(vmem, vmem),
        scratch_shapes=[
            pltpu.SMEM(live_groups.shape, jnp.int32),
            pltpu.VMEM((panels, samples), jnp.bfloat16),
            pltpu.VMEM((observers, panels), jnp.bfloat16),
            pltpu.VMEM((panels // CHUNK, observers, CHUNK), jnp.float32),
            pltpu.VMEM((observers, blocks), jnp.int32),
            pltpu.VMEM((observers, blocks), jnp.int32),
            pltpu.VMEM((observers, ROWS, blocks), jnp.bfloat16),
            pltpu.VMEM((observers, ROWS, blocks), jnp.bfloat16),
            pltpu.VMEM((observers, blocks, samples), jnp.bfloat16),
            pltpu.VMEM((samples // LANES + 1, observers * 8, LANES), jnp.float32),
            pltpu.SemaphoreType.DMA((4,)),
            pltpu.SemaphoreType.DMA((pieces,)),
        ],
        compiler_params=pltpu.CompilerParams(vmem_limit_bytes=60 * 1024 * 1024),
        name="far_partial",
    )(live_groups, loading, green, delays, offsets)


def shards(loading, green, delays, offsets, live_groups):
    main, tail = far_partial(loading, green, delays, offsets, live_groups)
    samples = main.shape[1]
    carried = passed_along(tail, "slab", 1)
    part = main + jnp.pad(carried, ((0, 0), (0, samples - LAGS)))
    sectors = lax.axis_size("panel")
    reach = 1
    while reach < sectors:
        part = part + lax.ppermute(part, "panel", [(i, i ^ reach) for i in range(sectors)])
        reach *= 2
    return part


def solution(mesh):
    placed = (
        P(("case", "panel"), "slab"),
        P(("case", "obs"), "panel"),
        P(("case", "obs"), "panel"),
        P(("case", "obs"), "panel"),
        P("case"),
    )
    return jax.shard_map(
        shards, mesh=mesh, in_specs=placed, out_specs=P(("case", "obs"), "slab"), check_vma=False
    )
```

time: 135 us -> 36.3 us (0.27)
  local copies, waits for them, and re-layouts: 61 us -> 0 us
  blocking collectives: 46.4 us -> 0 us
  Pallas kernels: 0 us -> 15.3 us
  matrix products: 12.8 us -> 0 us
  starting transfers between devices: 4.84 us -> 14 us
  waiting for transfers between devices: 1.43 us -> 5.42 us
  other arithmetic: 4.86 us -> 1.39 us
  loops' own time: 2.97 us -> 0 us
    psum x1 -> x0, blocking collectives: 46.4 us -> none  [shards(): signal = lax.psum(local_part, 'panel')]
    reshape x3 -> x0, local copies, waits for them, and re-layouts: 25.1 us -> none  [skew_sum(): padded.reshape(observers, lag_count * row_width)]
    pallas_call x0 -> x1, Pallas kernels: none -> 15.3 us  [far_partial(): pl.pallas_call(functools.partial(far_kernel, groups), out_shape=(jax.Shap...]
    pad x3 -> x0, local copies, waits for them, and re-layouts: 13.3 us -> none  [skew_sum(): padded = jnp.pad(lagged, ((0, 0), (0, 0), (0, lag_count + 1)))]
    dot_general x6 -> x0, matrix products: 12.8 us -> none  [the longest x3 10.5 us: group_signal(): jnp.einsum('olb,bot->olt', lag_table, block_signal, preferred_element_typ...]
    dynamic_slice x13 -> x0, local copies, waits for them, and re-layouts: 11 us -> none  [the longest x3 3.9 us: slice_group(): lax.dynamic_slice_in_dim(loading, start, group_panels, 0)]
    ppermute x0 -> x2, starting transfers between devices: none -> 9.12 us  [shards(): lax.ppermute(part, 'panel', [(i, i ^ reach) for i in range(sectors)])]
    slice x7 -> x0, local copies, waits for them, and re-layouts: 8.36 us -> none  [the longest x6 8.35 us: skew_sum(): padded.reshape(observers, lag_count * row_width)]
  transfers between devices with their start and end apart: 1 -> 3, of which waited for: 1 -> 3; matrix products, arithmetic and copies ran while one was open for 0% -> 0% of each run, Pallas kernels for 0% -> 0%
where the time goes in v1:
time: 36.3 us; the launch traced here: 36.1 us
  Pallas kernels  15.3 us (42%)
  starting transfers between devices  14 us (39%)
  waiting for transfers between devices  5.42 us (15%)
  other arithmetic  1.39 us (4%)
    pallas_call x1, Pallas kernels, far_partial(): pl.pallas_call(functools.partial(far_kernel, groups), out_shape=(jax.Shap...  15.3 us
    ppermute x2, starting transfers between devices, shards(): lax.ppermute(part, 'panel', [(i, i ^ reach) for i in range(sectors)])  9.12 us
    ppermute x1, starting transfers between devices, passed_along(): return lax.ppermute(block, axis, route)  4.84 us
    ppermute x2, waiting for transfers between devices, shards(): lax.ppermute(part, 'panel', [(i, i ^ reach) for i in range(sectors)])  3.78 us
    ppermute x1, waiting for transfers between devices, passed_along(): return lax.ppermute(block, axis, route)  1.64 us
    add x1, other arithmetic, shards(): part = main + jnp.pad(carried, ((0, 0), (0, samples - LAGS)))  0.76 us
  transfers between devices with their start and end apart: 3, of which 3 were waited for; matrix products, arithmetic and copies ran while one was open for 0% of the time, Pallas kernels for 0%

profile of v1, /device:TPU:0, one launch (start us, length us, event | category | flops | bytes accessed | tf_op | source)
XLA Modules:
  0.0 36.1 jit_solution(8037320627614566535)
XLA Ops:
  0.0 15.3 %far_partial.1 = (f32[32,256]{1,0:T(8,128)}, f32[32,128]{1,0:T(8,128)}) custom-call(s32[4]{0:T(128)} %live_hbm.1, bf16[8192,256]{1,0:T(8,128)(2,1)} %load_hbm.1, bf16[32,8192]{1,0:T(8,128)(2,1)} %green_hbm.1, s32[32,512]{1,0:T(8,128)} %delay_hbm.1, s32[32,512]{1,0:T(8,128)} %offset_hbm.1), custom_call_target="tpu_custom_call" | custom-call | tf_op jit(solution)/shard_map/far_partial/pallas_call | solution.py:173
  15.3 4.8 %collective-permute-start = (f32[32,128]{1,0:T(8,128)}, f32[32,128]{1,0:T(8,128)S(1)}, u32[]{:S(2)}, u32[]{:S(2)}) collective-permute-start(f32[32,128]{1,0:T(8,128)} %get-tuple-element.8), channel_id=1, source_target_pairs={{0,2},{1,3},{4,6},{5,7},{8,10},{9,11},{12,14},{13,15},{16,18},{17,... | collective-permute-start | bytes 49160 | tf_op jit(solution)/shard_map/ppermute | solution.py:22
  20.2 1.6 %collective-permute-done = f32[32,128]{1,0:T(8,128)S(1)} collective-permute-done((f32[32,128]{1,0:T(8,128)}, f32[32,128]{1,0:T(8,128)S(1)}, u32[]{:S(2)}, u32[]{:S(2)}) %collective-permute-start) | collective-permute-done | bytes 16416 | tf_op jit(solution)/shard_map/ppermute | solution.py:22
  21.8 0.8 %pad_add_fusion = f32[32,256]{1,0:T(8,128)S(1)} fusion(f32[32,256]{1,0:T(8,128)} %get-tuple-element.7, f32[32,128]{1,0:T(8,128)S(1)} %collective-permute-done), kind=kLoop, calls=%fused_computation | loop fusion | flops 8192 | bytes 81920 | tf_op jit(solution)/shard_map/add | solution.py:204
  22.6 6.1 %collective-permute-start.1 = (f32[32,256]{1,0:T(8,128)S(1)}, f32[32,256]{1,0:T(8,128)S(1)}, u32[]{:S(2)}, u32[]{:S(2)}) collective-permute-start(f32[32,256]{1,0:T(8,128)S(1)} %pad_add_fusion), channel_id=1, source_target_pairs={{0,4},{4,0},{8,12},{12,8},{1,5},{5,1},{9,13},{13,9},{2,6},{6,2},{1... | collective-permute-start | bytes 98312 | tf_op jit(solution)/shard_map/ppermute | solution.py:208
  28.6 1.9 %collective-permute-done.1 = f32[32,256]{1,0:T(8,128)S(1)} collective-permute-done((f32[32,256]{1,0:T(8,128)S(1)}, f32[32,256]{1,0:T(8,128)S(1)}, u32[]{:S(2)}, u32[]{:S(2)}) %collective-permute-start.1) | collective-permute-done | bytes 32800 | tf_op jit(solution)/shard_map/ppermute | solution.py:208
  30.5 3.0 %collective-permute-start.2 = (f32[32,256]{1,0:T(8,128)S(1)}, f32[32,256]{1,0:T(8,128)S(1)}, u32[]{:S(2)}, u32[]{:S(2)}) collective-permute-start(f32[32,256]{1,0:T(8,128)S(1)} %add.12), channel_id=1, source_target_pairs={{0,8},{4,12},{8,0},{12,4},{1,9},{5,13},{9,1},{13,5},{2,10},{6,14},... | collective-permute-start | bytes 98312 | tf_op jit(solution)/shard_map/ppermute | solution.py:208
  33.6 1.9 %collective-permute-done.2 = f32[32,256]{1,0:T(8,128)S(1)} collective-permute-done((f32[32,256]{1,0:T(8,128)S(1)}, f32[32,256]{1,0:T(8,128)S(1)}, u32[]{:S(2)}, u32[]{:S(2)}) %collective-permute-start.2) | collective-permute-done | bytes 32800 | tf_op jit(solution)/shard_map/ppermute | solution.py:208
  35.5 0.6 %add.13 = f32[32,256]{1,0:T(8,128)} add(f32[32,256]{1,0:T(8,128)S(1)} %add.12, f32[32,256]{1,0:T(8,128)S(1)} %collective-permute-done.2) | non-fusion elementwise | flops 8192 | bytes 98304 | tf_op jit(solution)/shard_map/add | solution.py:208
  (1 shorter events, 0.0 us)
Async XLA Ops:
  15.3 6.5 %collective-permute-start = (f32[32,128]{1,0:T(8,128)}, f32[32,128]{1,0:T(8,128)S(1)}, u32[]{:S(2)}, u32[]{:S(2)}) collective-permute-start(f32[32,128]{1,0:T(8,128)} %get-tuple-element.8), channel_id=1, source_target_pairs={{0,2},{1,3},{4,6},{5,7},{8,10},{9,11},{12,14},{13,15},{16,18},{17,... | collective-permute-start | bytes 49160 | tf_op jit(solution)/shard_map/ppermute | solution.py:22
  22.6 8.0 %collective-permute-start.1 = (f32[32,256]{1,0:T(8,128)S(1)}, f32[32,256]{1,0:T(8,128)S(1)}, u32[]{:S(2)}, u32[]{:S(2)}) collective-permute-start(f32[32,256]{1,0:T(8,128)S(1)} %pad_add_fusion), channel_id=1, source_target_pairs={{0,4},{4,0},{8,12},{12,8},{1,5},{5,1},{9,13},{13,9},{2,6},{6,2},{1... | collective-permute-start | bytes 98312 | tf_op jit(solution)/shard_map/ppermute | solution.py:208
  30.5 4.9 %collective-permute-start.2 = (f32[32,256]{1,0:T(8,128)S(1)}, f32[32,256]{1,0:T(8,128)S(1)}, u32[]{:S(2)}, u32[]{:S(2)}) collective-permute-start(f32[32,256]{1,0:T(8,128)S(1)} %add.12), channel_id=1, source_target_pairs={{0,8},{4,12},{8,0},{12,4},{1,9},{5,13},{9,1},{13,5},{2,10},{6,14},... | collective-permute-start | bytes 98312 | tf_op jit(solution)/shard_map/ppermute | solution.py:208

commit v2 on v1

--- a/solution.py
+++ b/solution.py
@@ -74,12 +74,13 @@
         pltpu.make_async_copy(load_hbm.at[pl.ds(i * piece, piece)], load_v.at[pl.ds(i * piece, piece)], load_sem.at[i])
         for i in range(pieces)
     ]
-    for copy in loads:
-        copy.start()
+    loads[0].start()
 
     weights = weight_lanes()
     for copy in small[:3]:
         copy.wait()
+    for copy in loads[1:]:
+        copy.start()
     count = live_s[lax.axis_index("panel")]
     live_pairs = (count + 1) // 2
 
@@ -108,28 +109,39 @@
     small[3].wait()
     for c in range(panels // CHUNK):
         green_f[c] = green_v[:, c * CHUNK:(c + 1) * CHUNK].astype(jnp.float32)
-    for copy in loads:
-        copy.wait()
-
     own = lax.broadcasted_iota(jnp.int32, (ROWS, CHUNK), 1) // BP == lax.broadcasted_iota(jnp.int32, (ROWS, CHUNK), 0)
     own = own.astype(jnp.float32).astype(jnp.bfloat16)
 
-    def first(c, carry):
-        spread = []
-        for o in range(observers):
-            line = jnp.broadcast_to(green_f[c, o:o + 1, :], (ROWS, CHUNK)).astype(jnp.bfloat16)
-            spread.append(line * own)
-        block = jnp.dot(
-            jnp.concatenate(spread, 0),
-            load_v[pl.ds(pl.multiple_of(c * CHUNK, CHUNK), CHUNK), :],
-            preferred_element_type=jnp.float32,
-        ).astype(jnp.bfloat16)
-        at = pl.ds(pl.multiple_of(c * chunk_blocks, chunk_blocks), chunk_blocks)
-        for o in range(observers):
-            sig_v[o, at, :] = block[o * ROWS:(o + 1) * ROWS]
-        return carry
-
-    lax.fori_loop(0, live_pairs * (2 * GB // chunk_blocks), first, 0)
+    per = piece // CHUNK
+
+    def piece_here(i):
+        pltpu.make_async_copy(load_hbm.at[pl.ds(0, piece)], load_v.at[pl.ds(0, piece)], load_sem.at[i]).wait()
+
+    def first(i, carry):
+        piece_here(i)
+        for c in range(per):
+            chunk = i * per + c
+            spread = []
+            for o in range(observers):
+                line = jnp.broadcast_to(green_f[chunk, o:o + 1, :], (ROWS, CHUNK)).astype(jnp.bfloat16)
+                spread.append(line * own)
+            block = jnp.dot(
+                jnp.concatenate(spread, 0),
+                load_v[pl.ds(pl.multiple_of(chunk * CHUNK, CHUNK), CHUNK), :],
+                preferred_element_type=jnp.float32,
+            ).astype(jnp.bfloat16)
+            at = pl.ds(pl.multiple_of(chunk * chunk_blocks, chunk_blocks), chunk_blocks)
+            for o in range(observers):
+                sig_v[o, at, :] = block[o * ROWS:(o + 1) * ROWS]
+        return carry
+
+    def unused(i, carry):
+        piece_here(i)
+        return carry
+
+    wanted = live_pairs * 2
+    lax.fori_loop(0, wanted, first, 0)
+    lax.fori_loop(wanted, pieces, unused, 0)
 
     def second(depth, o, carry):
         taps = taps_v[o, :, :depth]
@@ -150,7 +162,7 @@
     for pair in range(1, pairs + 1):
         @pl.when(live_pairs == pair)
         def _():
-            lax.fori_loop(0, observers, functools.partial(second, pair * 2 * GB), 0, unroll=2)
+            lax.fori_loop(0, observers, functools.partial(second, pair * 2 * GB), 0, unroll=observers // 2)
 
     tiles_out = samples // LANES + 1
     total = [part_v[t, pl.ds(0, observers, stride=8), :] for t in range(tiles_out)]
@@ -167,7 +179,8 @@
     observers = green.shape[0]
     blocks = panels // BP
     groups = blocks // GB
-    pieces = panels // CHUNK // 2
+    pieces = groups
+    operands = (live_groups, loading, green, delays, offsets)
     far = pl.BlockSpec(memory_space=pltpu.HBM)
     vmem = pl.BlockSpec(memory_space=pltpu.VMEM)
     return pl.pallas_call(
@@ -192,9 +205,9 @@
             pltpu.SemaphoreType.DMA((4,)),
             pltpu.SemaphoreType.DMA((pieces,)),
         ],
-        compiler_params=pltpu.CompilerParams(vmem_limit_bytes=60 * 1024 * 1024),
+        compiler_params=pltpu.CompilerParams(vmem_limit_bytes=24 * 1024 * 1024),
         name="far_partial",
-    )(live_groups, loading, green, delays, offsets)
+    )(*[pltpu.with_memory_space_constraint(x, pltpu.HBM) for x in operands])
 
 
 def shards(loading, green, delays, offsets, live_groups):

time: 36.3 us -> 23.3 us (0.64)
  Pallas kernels: 15.3 us -> 5.99 us
  starting transfers between devices: 14 us -> 11.1 us
  other arithmetic: 1.39 us -> 0.63 us
    pallas_call x1, Pallas kernels: 15.3 us -> 5.99 us  [far_partial(): pl.pallas_call(functools.partial(far_kernel, groups), out_shape=(jax.Shap...]
    ppermute x2, starting transfers between devices: 9.12 us -> 6.3 us  [shards(): lax.ppermute(part, 'panel', [(i, i ^ reach) for i in range(sectors)])]
    add x1, other arithmetic: 0.76 us -> 0.01 us  [shards(): part = main + jnp.pad(carried, ((0, 0), (0, samples - LAGS)))]
where the time goes in v2:
time: 23.3 us; the launch traced here: 23 us
  starting transfers between devices  11.1 us (48%)
  Pallas kernels  5.99 us (26%)
  waiting for transfers between devices  5.21 us (22%)
  other arithmetic  0.63 us (3%)
    ppermute x2, starting transfers between devices, shards(): lax.ppermute(part, 'panel', [(i, i ^ reach) for i in range(sectors)])  6.3 us
    pallas_call x1, Pallas kernels, far_partial(): pl.pallas_call(functools.partial(far_kernel, groups), out_shape=(jax.Shap...  5.99 us
    ppermute x1, starting transfers between devices, passed_along(): return lax.ppermute(block, axis, route)  4.85 us
    ppermute x2, waiting for transfers between devices, shards(): lax.ppermute(part, 'panel', [(i, i ^ reach) for i in range(sectors)])  3.78 us
    ppermute x1, waiting for transfers between devices, passed_along(): return lax.ppermute(block, axis, route)  1.43 us
    add x2, other arithmetic, shards(): part + lax.ppermute(part, 'panel', [(i, i ^ reach) for i in range(sectors)])  0.62 us
  transfers between devices with their start and end apart: 3, of which 3 were waited for; matrix products, arithmetic and copies ran while one was open for 0% of the time, Pallas kernels for 0%

profile of v2, /device:TPU:0, one launch (start us, length us, event | category | flops | bytes accessed | tf_op | source)
XLA Modules:
  0.0 23.0 jit_solution(11717800960852197188)
XLA Ops:
  0.0 6.0 %far_partial.1 = (f32[32,256]{1,0:T(8,128)S(1)}, f32[32,128]{1,0:T(8,128)S(1)}) custom-call(s32[4]{0:T(128)} %live_hbm.1, bf16[8192,256]{1,0:T(8,128)(2,1)} %load_hbm.1, bf16[32,8192]{1,0:T(8,128)(2,1)} %green_hbm.1, s32[32,512]{1,0:T(8,128)} %delay_hbm.1, s32[32,512]{1,0:T(8,128)} %offset_hbm.1), custom_call_target="tpu_custom_call" | custom-call | tf_op jit(solution)/shard_map/far_partial/pallas_call | solution.py:186
  6.0 4.9 %collective-permute-start = (f32[32,128]{1,0:T(8,128)S(1)}, f32[32,128]{1,0:T(8,128)S(1)}, u32[]{:S(2)}, u32[]{:S(2)}) collective-permute-start(f32[32,128]{1,0:T(8,128)S(1)} %get-tuple-element.8), channel_id=1, source_target_pairs={{0,2},{1,3},{4,6},{5,7},{8,10},{9,11},{12,14},{13,15},{16,18},{17,... | collective-permute-start | bytes 49160 | tf_op jit(solution)/shard_map/ppermute | solution.py:22
  10.9 1.4 %collective-permute-done = f32[32,128]{1,0:T(8,128)S(1)} collective-permute-done((f32[32,128]{1,0:T(8,128)S(1)}, f32[32,128]{1,0:T(8,128)S(1)}, u32[]{:S(2)}, u32[]{:S(2)}) %collective-permute-start) | collective-permute-done | bytes 16416 | tf_op jit(solution)/shard_map/ppermute | solution.py:22
  12.3 3.3 %collective-permute-start.1 = (f32[32,256]{1,0:T(8,128)S(1)}, f32[32,256]{1,0:T(8,128)S(1)}, u32[]{:S(2)}, u32[]{:S(2)}) collective-permute-start(f32[32,256]{1,0:T(8,128)S(1)} %pad_add_fusion), channel_id=1, source_target_pairs={{0,4},{4,0},{8,12},{12,8},{1,5},{5,1},{9,13},{13,9},{2,6},{6,2},{1... | collective-permute-start | bytes 98312 | tf_op jit(solution)/shard_map/ppermute | solution.py:221
  15.6 1.9 %collective-permute-done.1 = f32[32,256]{1,0:T(8,128)S(1)} collective-permute-done((f32[32,256]{1,0:T(8,128)S(1)}, f32[32,256]{1,0:T(8,128)S(1)}, u32[]{:S(2)}, u32[]{:S(2)}) %collective-permute-start.1) | collective-permute-done | bytes 32800 | tf_op jit(solution)/shard_map/ppermute | solution.py:221
  17.5 3.0 %collective-permute-start.2 = (f32[32,256]{1,0:T(8,128)S(1)}, f32[32,256]{1,0:T(8,128)S(1)}, u32[]{:S(2)}, u32[]{:S(2)}) collective-permute-start(f32[32,256]{1,0:T(8,128)S(1)} %add.12), channel_id=1, source_target_pairs={{0,8},{4,12},{8,0},{12,4},{1,9},{5,13},{9,1},{13,5},{2,10},{6,14},... | collective-permute-start | bytes 98312 | tf_op jit(solution)/shard_map/ppermute | solution.py:221
  20.5 1.9 %collective-permute-done.2 = f32[32,256]{1,0:T(8,128)S(1)} collective-permute-done((f32[32,256]{1,0:T(8,128)S(1)}, f32[32,256]{1,0:T(8,128)S(1)}, u32[]{:S(2)}, u32[]{:S(2)}) %collective-permute-start.2) | collective-permute-done | bytes 32800 | tf_op jit(solution)/shard_map/ppermute | solution.py:221
  22.4 0.6 %add.13 = f32[32,256]{1,0:T(8,128)} add(f32[32,256]{1,0:T(8,128)S(1)} %add.12, f32[32,256]{1,0:T(8,128)S(1)} %collective-permute-done.2) | non-fusion elementwise | flops 8192 | bytes 98304 | tf_op jit(solution)/shard_map/add | solution.py:221
  (2 shorter events, 0.0 us)
Async XLA Ops:
  6.0 6.3 %collective-permute-start = (f32[32,128]{1,0:T(8,128)S(1)}, f32[32,128]{1,0:T(8,128)S(1)}, u32[]{:S(2)}, u32[]{:S(2)}) collective-permute-start(f32[32,128]{1,0:T(8,128)S(1)} %get-tuple-element.8), channel_id=1, source_target_pairs={{0,2},{1,3},{4,6},{5,7},{8,10},{9,11},{12,14},{13,15},{16,18},{17,... | collective-permute-start | bytes 49160 | tf_op jit(solution)/shard_map/ppermute | solution.py:22
  12.3 5.2 %collective-permute-start.1 = (f32[32,256]{1,0:T(8,128)S(1)}, f32[32,256]{1,0:T(8,128)S(1)}, u32[]{:S(2)}, u32[]{:S(2)}) collective-permute-start(f32[32,256]{1,0:T(8,128)S(1)} %pad_add_fusion), channel_id=1, source_target_pairs={{0,4},{4,0},{8,12},{12,8},{1,5},{5,1},{9,13},{13,9},{2,6},{6,2},{1... | collective-permute-start | bytes 98312 | tf_op jit(solution)/shard_map/ppermute | solution.py:221
  17.5 4.9 %collective-permute-start.2 = (f32[32,256]{1,0:T(8,128)S(1)}, f32[32,256]{1,0:T(8,128)S(1)}, u32[]{:S(2)}, u32[]{:S(2)}) collective-permute-start(f32[32,256]{1,0:T(8,128)S(1)} %add.12), channel_id=1, source_target_pairs={{0,8},{4,12},{8,0},{12,4},{1,9},{5,13},{9,1},{13,5},{2,10},{6,14},... | collective-permute-start | bytes 98312 | tf_op jit(solution)/shard_map/ppermute | solution.py:221
